TPU v7x, 512 devices: a whole 4x4x16 slice. The times are simulated.
512 devices in a mesh: row: 64 (over x, z), col: 8 (over y, core).
Axes of the slice: x: 4, y: 4, z: 16, core: 2. Of those that a mesh axis runs over, the one named last changes fastest.
Arguments:
- kelvin_start: float32 [512, 512, 128], P('row', 'col'), may hold values from 1 to 2.5
- mass_ratio: float32 [512, 512, 128], P('row', 'col'), may hold values from 0.6 to 1
- material_region_labels: int32 [512, 512], P('row', 'col'), may hold values from 0 to 7
- pristine_conductivity: float32 [8], replicated, may hold values from 0.5 to 2
- burnt_conductivity: float32 [8], replicated, may hold values from 0.5 to 2
- burnt_mass_ratio: float32 [8], replicated, may hold values from 0.25 to 0.5
- arrhenius_prefactor: float32 [8], replicated, may hold values from 1 to 30
- onset_kelvin: float32 [8], replicated, may hold values from 2 to 6
- exchange_film_strength: float32 [64, 8, 64, 128], P('row', 'col'), may hold values from 0.25 to 4
- stagnation_kelvin: float32 [64, 8, 64, 128], P('row', 'col'), may hold values from 2 to 6
- receiving_element: int32 [64, 8, 64, 128], P('row', 'col'), may hold values from 0 to 511
- occupied_slot_totals: int32 [64, 8, 64], P('row', 'col'), may hold values from 16 to 128, as said below
Outputs:
- kelvin_after: float32 [512, 512, 128], P('row', 'col')
- mass_ratio_after: float32 [512, 512, 128], P('row', 'col')
Inputs may be any that keep to these rules, and one draw needn't show every extreme that they name: `occupied_slot_totals`: live slots come first in each block; in every col one destination tile receives 128 live faces from every source; slots at or past the count hold arbitrary values. `receiving_element`: cell i * 64 + j is row i and column j of the destination tile.
All inputs are finite; a program needn't handle non-finite values.
Results may differ from a plain program's by a relative error of at most 0.0003.
Values sent between devices are 32-bit elements; how exact they have to be, the bound alone decides.
A program may use at most 64 MiB of HBM per device.

v0:
```python
import jax
import jax.numpy as jnp
from jax import lax
from jax.sharding import PartitionSpec as P

R_X = 32
R_Y = 64
R_Z = 1024
EXTERIOR_SHARE = 16
HEAT_OF_PYROLYSIS = 0.3


def take_part(values, first_index, end_index, stride, solve_dim):
    return lax.slice_in_dim(values, first_index, end_index, stride, solve_dim)


def extend_end(values, filler, solve_dim):
    new_shape = list(values.shape)
    new_shape[solve_dim] = 1
    return jnp.concatenate([values, jnp.full(new_shape, filler, values.dtype)], solve_dim)


def merge_halves(even_value, odd_value, odd_count, solve_dim):
    even_head = take_part(even_value, 0, odd_count, 1, solve_dim)
    paired = jnp.stack([even_head, odd_value], solve_dim + 1)
    new_shape = list(even_head.shape)
    new_shape[solve_dim] = 2 * odd_count
    merged = paired.reshape(new_shape)
    return merged


def cyclic_solve(sub_diag, main_diag, super_diag, rights, solve_dim):
    length = main_diag.shape[solve_dim]
    if length == 1:
        return [vector / main_diag for vector in rights]
    odd_count = length // 2
    even_count = length - odd_count
    even_parts = [
        take_part(operand, 0, length, 2, solve_dim) for operand in (sub_diag, main_diag, super_diag)
    ]
    odd_parts = [
        take_part(operand, 1, length, 2, solve_dim) for operand in (sub_diag, main_diag, super_diag)
    ]
    even_rights = [take_part(vector, 0, length, 2, solve_dim) for vector in rights]
    odd_rights = [take_part(vector, 1, length, 2, solve_dim) for vector in rights]
    left_sub, left_main, left_super = [
        take_part(operand, 0, odd_count, 1, solve_dim) for operand in even_parts
    ]
    left_rights = [take_part(vector, 0, odd_count, 1, solve_dim) for vector in even_rights]
    right_sub = take_part(extend_end(even_parts[0], 0.0, solve_dim), 1, odd_count + 1, 1, solve_dim)
    right_main = take_part(
        extend_end(even_parts[1], 1.0, solve_dim), 1, odd_count + 1, 1, solve_dim
    )
    right_super = take_part(
        extend_end(even_parts[2], 0.0, solve_dim), 1, odd_count + 1, 1, solve_dim
    )
    right_rights = [
        take_part(extend_end(vector, 0.0, solve_dim), 1, odd_count + 1, 1, solve_dim)
        for vector in even_rights
    ]
    left_factor = -odd_parts[0] / left_main
    right_factor = -odd_parts[2] / right_main
    reduced_sub = left_factor * left_sub
    reduced_main = odd_parts[1] + left_factor * left_super + right_factor * right_sub
    reduced_super = right_factor * right_super
    reduced_rights = [
        odd_part + left_factor * left_part + right_factor * right_part
        for odd_part, left_part, right_part in zip(odd_rights, left_rights, right_rights)
    ]
    odd_solutions = cyclic_solve(
        reduced_sub, reduced_main, reduced_super, reduced_rights, solve_dim
    )
    results = []
    for even_part, odd_part in zip(even_rights, odd_solutions):
        edge_shape = list(odd_part.shape)
        edge_shape[solve_dim] = 1
        zero_plane = jnp.zeros(edge_shape, odd_part.dtype)
        padded = jnp.concatenate([zero_plane, odd_part, zero_plane], solve_dim)
        before = take_part(padded, 0, even_count, 1, solve_dim)
        after_vals = take_part(padded, 1, even_count + 1, 1, solve_dim)
        even_value = (even_part - even_parts[0] * before - even_parts[2] * after_vals) / even_parts[
            1
        ]
        results.append(merge_halves(even_value, odd_part, odd_count, solve_dim))
    return results


def sweep_coefficients(capacity, diffuse_thermal_energy, diffusion, solve_dim):
    length = diffuse_thermal_energy.shape[solve_dim]
    face_cond = 0.5 * (
        take_part(diffuse_thermal_energy, 0, length - 1, 1, solve_dim)
        + take_part(diffuse_thermal_energy, 1, length, 1, solve_dim)
    )
    edge_shape = list(diffuse_thermal_energy.shape)
    edge_shape[solve_dim] = 1
    zero_edge = jnp.zeros(edge_shape, diffuse_thermal_energy.dtype)
    sub_diag = -diffusion * jnp.concatenate([zero_edge, face_cond], solve_dim)
    super_diag = -diffusion * jnp.concatenate([face_cond, zero_edge], solve_dim)
    main_diag = capacity - sub_diag - super_diag
    return (sub_diag, main_diag, super_diag)


def solve_lines(pieces, diffusion, solve_dim):
    sub_diag, main_diag, super_diag = sweep_coefficients(pieces[1], pieces[2], diffusion, solve_dim)
    return cyclic_solve(sub_diag, main_diag, super_diag, [pieces[0]], solve_dim)[0]


def column_values(material_region_labels, property_arrays):
    matches = (
        material_region_labels[..., None]
        == jnp.arange(property_arrays[0].shape[0], dtype=jnp.int32)
    ).astype(jnp.float32)
    return [jnp.sum(matches * lookup, axis=-1)[..., None] for lookup in property_arrays]


def decompose_through_layers(
    kelvin_start,
    mass_ratio,
    material_region_labels,
    property_arrays,
    exterior_multiplier,
    exterior_flux_amount,
):
    virgin, charred, residue, rate_col, energy = column_values(
        material_region_labels, property_arrays
    )
    old_conduct = charred + (virgin - charred) * (mass_ratio - residue) / (1.0 - residue)
    thickness_dimension = kelvin_start.ndim - 1
    sub_diag, main_diag, super_diag = sweep_coefficients(
        mass_ratio, old_conduct, float(R_Z), thickness_dimension
    )
    main_diag = main_diag.at[..., 0].add(float(EXTERIOR_SHARE) * exterior_multiplier)
    forcing_vector = (
        (mass_ratio * kelvin_start).at[..., 0].add(float(EXTERIOR_SHARE) * exterior_flux_amount)
    )
    depth_temp = cyclic_solve(
        sub_diag, main_diag, super_diag, [forcing_vector], thickness_dimension
    )[0]
    extent = rate_col * jnp.exp(-energy / depth_temp)
    mass_ratio_after = residue + (mass_ratio - residue) * jnp.exp(-extent)
    warmed_fields = (
        depth_temp - HEAT_OF_PYROLYSIS * (mass_ratio - mass_ratio_after) / mass_ratio_after
    )
    diffuse_thermal_energy = charred + (virgin - charred) * (mass_ratio_after - residue) / (
        1.0 - residue
    )
    return (warmed_fields, mass_ratio_after, diffuse_thermal_energy)


def solve_x(pieces):
    return solve_lines(pieces, float(R_X), 0)


def sweep_trailing_lines(pieces):
    return solve_lines(pieces, float(R_Y), 1)


def per_device(
    kelvin_start,
    mass_ratio,
    material_region_labels,
    pristine_conductivity,
    burnt_conductivity,
    burnt_mass_ratio,
    arrhenius_prefactor,
    onset_kelvin,
    exchange_film_strength,
    stagnation_kelvin,
    receiving_element,
    occupied_slot_totals,
):
    patch_leading_extent, patch_trailing_extent, layer_number = kelvin_start.shape
    sources = lax.axis_size("row")
    cell_count = patch_leading_extent * patch_trailing_extent
    slot_index = jnp.arange(exchange_film_strength.shape[-1], dtype=jnp.int32)
    live_slots = (slot_index < occupied_slot_totals[..., None]).astype(jnp.float32)
    blending_shares = (exchange_film_strength * live_slots)[0, 0]
    flux_arriving = blending_shares * stagnation_kelvin[0, 0]
    targets = receiving_element[0, 0]
    offsets = jnp.arange(sources, dtype=jnp.int32)[:, None] * cell_count + targets
    flat_ids = offsets.reshape(-1)
    tile_weight = jax.ops.segment_sum(
        blending_shares.reshape(-1), flat_ids, num_segments=sources * cell_count
    )
    tile_heat = jax.ops.segment_sum(
        flux_arriving.reshape(-1), flat_ids, num_segments=sources * cell_count
    )
    exterior_multiplier, exterior_flux_amount = (
        lax.psum_scatter(tile_weight, "row", scatter_dimension=0, tiled=True),
        lax.psum_scatter(tile_heat, "row", scatter_dimension=0, tiled=True),
    )
    exterior_multiplier = exterior_multiplier.reshape(patch_leading_extent, patch_trailing_extent)
    exterior_flux_amount = exterior_flux_amount.reshape(patch_leading_extent, patch_trailing_extent)
    property_arrays = (
        pristine_conductivity,
        burnt_conductivity,
        burnt_mass_ratio,
        arrhenius_prefactor,
        onset_kelvin,
    )
    warmed_fields, mass_ratio_after, diffuse_thermal_energy = decompose_through_layers(
        kelvin_start,
        mass_ratio,
        material_region_labels,
        property_arrays,
        exterior_multiplier,
        exterior_flux_amount,
    )
    forcing_vector = mass_ratio_after * warmed_fields
    line_share = patch_trailing_extent * layer_number // sources
    flat_parts = (forcing_vector, mass_ratio_after, diffuse_thermal_energy)
    solved_x = solve_x(
        (
            lax.all_to_all(flat_parts[0], "row", split_axis=1, concat_axis=0, tiled=True),
            lax.all_to_all(flat_parts[1], "row", split_axis=1, concat_axis=0, tiled=True),
            lax.all_to_all(flat_parts[2], "row", split_axis=1, concat_axis=0, tiled=True),
        )
    )
    across = lax.all_to_all(solved_x, "row", split_axis=0, concat_axis=1, tiled=True)
    forcing_vector_other = mass_ratio_after * across
    solved_state = sweep_trailing_lines(
        (
            lax.all_to_all(forcing_vector_other, "col", split_axis=0, concat_axis=1, tiled=True),
            lax.all_to_all(mass_ratio_after, "col", split_axis=0, concat_axis=1, tiled=True),
            lax.all_to_all(diffuse_thermal_energy, "col", split_axis=0, concat_axis=1, tiled=True),
        )
    )
    kelvin_after = lax.all_to_all(solved_state, "col", split_axis=1, concat_axis=0, tiled=True)
    return (kelvin_after, mass_ratio_after)


def solution(mesh):
    return jax.shard_map(
        per_device,
        mesh=mesh,
        in_specs=(
            P("row", "col", None),
            P("row", "col", None),
            P("row", "col"),
            P(),
            P(),
            P(),
            P(),
            P(),
            P("row", "col", None, None),
            P("row", "col", None, None),
            P("row", "col", None, None),
            P("row", "col", None),
        ),
        out_specs=(P("row", "col", None), P("row", "col", None)),
        check_vma=False,
    )
```

profile of v0, /device:TPU:1, one launch (start us, length us, event | category | flops | bytes accessed | tf_op | source)
XLA Modules:
  0.0 658.0 jit_solution(1565937443796117026)
XLA Ops:
  8.8 57.7 %scatter_custom_fusion = f32[32768]{0:T(1024)} fusion(s32[8192]{0:T(1024)S(1)} %bitcast.253, f32[8192]{0:T(1024)S(1)} %get-tuple-element.52, f32[]{:T(128)} %constant.67.clone.1), kind=kCustom, calls=%fused_computation.156 | custom fusion | flops 8192 | bytes 131076 | tf_op jit(solution)/shard_map/scatter-add | solution.py:185
  66.5 57.6 %scatter_custom_fusion.1 = f32[32768]{0:T(1024)} fusion(s32[8192]{0:T(1024)S(1)} %bitcast.254, f32[8192]{0:T(1024)S(1)} %get-tuple-element.53, f32[]{:T(128)} %constant.67.clone.1), kind=kCustom, calls=%fused_computation.154 | custom fusion | flops 8192 | bytes 131076 | tf_op jit(solution)/shard_map/scatter-add | solution.py:182
  125.6 4.5 slice.1033
  130.1 4.5 slice.1025
  134.7 4.5 slice.1020
  139.2 4.5 slice.1022
  145.8 236.7 %all-reduce.121.cloned.1.call-done = (f32[32768]{0:T(1024)}, f32[32768]{0:T(1024)}) async-done(((f32[32768]{0:T(1024)}, f32[32768]{0:T(1024)}), (f32[32768]{0:T(1024)}, f32[32768]{0:T(1024)})) %all-reduce.121.cloned.1.call-update) | async-done | bytes 262160
  383.9 4.5 slice.1017
  388.4 4.5 slice.1021
  393.4 4.5 slice.1024
  397.9 4.5 slice.1032
  405.3 3.0 slice.1030
  410.6 3.0 slice.1044
  415.9 3.0 slice.1031
  421.2 3.0 slice.1037
  453.9 2.7 multiply_add_fusion.6
  465.1 2.5 multiply_add_fusion.4
  495.9 8.0 %all-to-all-start = ((f32[8,64,128]{2,0,1:T(8,128)}), f32[8,64,128]{2,0,1:T(8,128)S(1)}, u32[]{:S(2)}, u32[]{:S(2)}) async-start(f32[8,64,128]{2,0,1:T(8,128)} %copy.540), calls=%async_computation | async-start | bytes 524288 | tf_op jit(solution)/shard_map/all_to_all | solution.py:214
  507.7 11.8 %all-to-all-done = f32[8,64,128]{2,0,1:T(8,128)S(1)} async-done(((f32[8,64,128]{2,0,1:T(8,128)}), f32[8,64,128]{2,0,1:T(8,128)S(1)}, u32[]{:S(2)}, u32[]{:S(2)}) %all-to-all-start) | async-done | bytes 262176 | tf_op jit(solution)/shard_map/all_to_all | solution.py:214
  519.5 6.2 all-to-all-start.1
  527.5 13.6 %all-to-all-done.1 = f32[8,64,128]{2,0,1:T(8,128)S(1)} async-done(((f32[8,64,128]{2,0,1:T(8,128)}), f32[8,64,128]{2,0,1:T(8,128)S(1)}, u32[]{:S(2)}, u32[]{:S(2)}) %all-to-all-start.1) | async-done | bytes 262176 | tf_op jit(solution)/shard_map/all_to_all | solution.py:216
  541.2 6.4 all-to-all-start.2
  547.8 15.2 %all-to-all-done.2 = f32[8,64,128]{2,0,1:T(8,128)S(1)} async-done(((f32[8,64,128]{2,0,1:T(8,128)}), f32[8,64,128]{2,0,1:T(8,128)S(1)}, u32[]{:S(2)}, u32[]{:S(2)}) %all-to-all-start.2) | async-done | bytes 262176 | tf_op jit(solution)/shard_map/all_to_all | solution.py:215
  563.0 19.4 %all-to-all-start.5 = ((f32[8,64,128]{2,1,0:T(8,128)}), f32[8,64,128]{2,1,0:T(8,128)S(1)}, u32[]{:S(2)}, u32[]{:S(2)}) async-start(f32[8,64,128]{2,1,0:T(8,128)} %divide_add_fusion), calls=%async_computation.5 | async-start | bytes 524288 | tf_op jit(solution)/shard_map/all_to_all | solution.py:225
  585.9 3.0 all-to-all-done.5
  588.9 6.3 all-to-all-start.3
  595.3 18.6 %all-to-all-done.3 = f32[512,1,128]{2,1,0:T(1,128)S(1)} async-done(((f32[512,1,128]{2,1,0:T(1,128)}), f32[512,1,128]{2,1,0:T(1,128)S(1)}, u32[]{:S(2)}, u32[]{:S(2)}) %all-to-all-start.3) | async-done | bytes 262176 | tf_op jit(solution)/shard_map/all_to_all | solution.py:219
  613.9 6.7 %all-to-all-start.6 = ((f32[8,64,128]{2,1,0:T(8,128)}), f32[8,64,128]{2,1,0:T(8,128)S(1)}, u32[]{:S(2)}, u32[]{:S(2)}) async-start(f32[8,64,128]{2,1,0:T(8,128)} %get-tuple-element.163), calls=%async_computation.6 | async-start | bytes 524288 | tf_op jit(solution)/shard_map/all_to_all | solution.py:224
  622.3 4.8 all-to-all-done.6
  627.1 4.4 all-to-all-start.4
  632.1 5.9 all-to-all-done.4
  640.3 9.9 %all_to_all.120 = f32[1,512,128]{2,0,1:T(1,128)S(1)} all-to-all(f32[1,512,128]{2,0,1:T(1,128)S(1)} %bitcast.222), channel_id=1, replica_groups=mesh['row'=64,'col'=8] {'col'}, dimensions={1} | all-to-all | bytes 524288 | tf_op jit(solution)/shard_map/all_to_all | solution.py:228
  (355 shorter events, 95.9 us)
Async XLA Ops:
  7.2 0.8 copy-start.16
  7.2 375.3 %all-reduce.121.cloned.1.call-start = ((), (), s32[]{:S(2)}) async-start(), calls=%async_computation.8 | async-start | bytes 524288
  7.9 0.8 copy-start.17
  7.9 0.8 copy-start.18
  8.0 0.7 copy-start.20
  8.8 116.2 %copy-start.11 = (f32[8,64,128]{2,1,0:T(8,128)S(1)}, f32[8,64,128]{2,1,0:T(8,128)}, u32[]{:S(2)}) copy-start(f32[8,64,128]{2,1,0:T(8,128)} %param.17) | copy-start | bytes 786436
  8.8 116.2 %copy-start.15 = (f32[8,64,128]{2,1,0:T(8,128)S(1)}, f32[8,64,128]{2,1,0:T(8,128)}, u32[]{:S(2)}) copy-start(f32[8,64,128]{2,1,0:T(8,128)} %param.16) | copy-start | bytes 786436
  124.1 0.7 copy-start.22
  124.1 0.7 copy-start.23
  124.1 0.7 copy-start.24
  124.1 0.7 copy-start.25
  472.9 1.1 copy-start.9
  476.4 1.0 copy-start.10
  479.3 2.0 copy-start.7
  479.3 2.0 copy-start.8
  481.3 4.1 copy-start.5
  481.3 4.1 copy-start.6
  483.4 2.0 copy-start.3
  483.4 2.0 copy-start.4
  487.3 0.9 copy-start.13
  488.3 1.0 copy-start.1
  488.3 1.0 copy-start.2
  488.5 1.0 copy-start
  490.4 0.9 copy-start.14
  493.1 1.0 copy-start.12
  495.9 23.6 %all-to-all-start = ((f32[8,64,128]{2,0,1:T(8,128)}), f32[8,64,128]{2,0,1:T(8,128)S(1)}, u32[]{:S(2)}, u32[]{:S(2)}) async-start(f32[8,64,128]{2,0,1:T(8,128)} %copy.540), calls=%async_computation | async-start | bytes 524288 | tf_op jit(solution)/shard_map/all_to_all | solution.py:214
  519.5 21.7 %all-to-all-start.1 = ((f32[8,64,128]{2,0,1:T(8,128)}), f32[8,64,128]{2,0,1:T(8,128)S(1)}, u32[]{:S(2)}, u32[]{:S(2)}) async-start(f32[8,64,128]{2,0,1:T(8,128)} %copy.541), calls=%async_computation.1 | async-start | bytes 524288 | tf_op jit(solution)/shard_map/all_to_all | solution.py:216
  541.2 21.8 %all-to-all-start.2 = ((f32[8,64,128]{2,0,1:T(8,128)}), f32[8,64,128]{2,0,1:T(8,128)S(1)}, u32[]{:S(2)}, u32[]{:S(2)}) async-start(f32[8,64,128]{2,0,1:T(8,128)} %copy.542), calls=%async_computation.2 | async-start | bytes 524288 | tf_op jit(solution)/shard_map/all_to_all | solution.py:215
  563.0 25.9 %all-to-all-start.5 = ((f32[8,64,128]{2,1,0:T(8,128)}), f32[8,64,128]{2,1,0:T(8,128)S(1)}, u32[]{:S(2)}, u32[]{:S(2)}) async-start(f32[8,64,128]{2,1,0:T(8,128)} %divide_add_fusion), calls=%async_computation.5 | async-start | bytes 524288 | tf_op jit(solution)/shard_map/all_to_all | solution.py:225
  588.9 25.0 %all-to-all-start.3 = ((f32[512,1,128]{2,1,0:T(1,128)}), f32[512,1,128]{2,1,0:T(1,128)S(1)}, u32[]{:S(2)}, u32[]{:S(2)}) async-start(f32[512,1,128]{2,1,0:T(1,128)} %bitcast.85), calls=%async_computation.3 | async-start | bytes 524288 | tf_op jit(solution)/shard_map/all_to_all | solution.py:219
  613.9 13.2 %all-to-all-start.6 = ((f32[8,64,128]{2,1,0:T(8,128)}), f32[8,64,128]{2,1,0:T(8,128)S(1)}, u32[]{:S(2)}, u32[]{:S(2)}) async-start(f32[8,64,128]{2,1,0:T(8,128)} %get-tuple-element.163), calls=%async_computation.6 | async-start | bytes 524288 | tf_op jit(solution)/shard_map/all_to_all | solution.py:224
  627.1 10.9 %all-to-all-start.4 = ((f32[8,64,128]{2,1,0:T(8,128)}), f32[8,64,128]{2,1,0:T(8,128)S(1)}, u32[]{:S(2)}, u32[]{:S(2)}) async-start(f32[8,64,128]{2,1,0:T(8,128)} %bitcast_multiply_fusion), calls=%async_computation.4 | async-start | bytes 524288 | tf_op jit(solution)/shard_map/all_to_all | solution.py:223
  (2 other events, 1.4 us)
Sparse Core Ops, SparseCore 0:
  124.3 258.1 all-reduce.120
where the time goes:
time: 667 us; the launch traced here: 658 us
  waiting for transfers between devices  310 us (46%)
  other arithmetic  142 us (21%)
  local copies, waits for them, and re-layouts  122 us (18%)
  starting transfers between devices  57.4 us (9%)
  between operations  16.5 us (2%)
  blocking collectives  9.95 us (1%)
    unnamed x2, waiting for transfers between devices  237 us
    slice x177, local copies, waits for them, and re-layouts, take_part(): return lax.slice_in_dim(values, first_index, end_index, stride, solve_dim)  101 us
    scatter-add x1, other arithmetic, per_device(): jax.ops.segment_sum(flux_arriving.reshape(-1), flat_ids, num_segments=sou...  57.7 us
    scatter-add x1, other arithmetic, per_device(): jax.ops.segment_sum(blending_shares.reshape(-1), flat_ids, num_segments=s...  57.6 us
    all_to_all x1, starting transfers between devices, per_device(): lax.all_to_all(diffuse_thermal_energy, 'col', split_axis=0, concat_axis=1...  19.4 us
    all_to_all x1, waiting for transfers between devices, per_device(): lax.all_to_all(solved_x, 'row', split_axis=0, concat_axis=1, tiled=True)  18.6 us
    all_to_all x1, waiting for transfers between devices, per_device(): lax.all_to_all(flat_parts[1], 'row', split_axis=1, concat_axis=0, tiled=T...  15.2 us
    all_to_all x1, waiting for transfers between devices, per_device(): lax.all_to_all(flat_parts[2], 'row', split_axis=1, concat_axis=0, tiled=T...  13.6 us
  transfers between devices with their start and end apart: 8, of which 8 were waited for; matrix products, arithmetic and copies ran while one was open for 5% of the time, Pallas kernels for 0%

commit v1 on v0

--- a/solution.py
+++ b/solution.py
@@ -8,6 +8,22 @@
 R_Z = 1024
 EXTERIOR_SHARE = 16
 HEAT_OF_PYROLYSIS = 0.3
+
+
+def swapped_with_each(value, axis, split, join):
+    ways, here = (lax.axis_size(axis), lax.axis_index(axis))
+    width = value.shape[split] // ways
+    lengths = list(value.shape)
+    lengths[split] = width
+    height = lengths[join]
+    lengths[join] = height * ways
+    full = jnp.zeros(lengths, value.dtype)
+    for mask in range(ways):
+        part = lax.dynamic_slice_in_dim(value, (here ^ mask) * width, width, axis=split)
+        if mask:
+            part = lax.ppermute(part, axis, [(d, d ^ mask) for d in range(ways)])
+        full = lax.dynamic_update_slice_in_dim(full, part, (here ^ mask) * height, axis=join)
+    return full
 
 
 def take_part(values, first_index, end_index, stride, solve_dim):
@@ -222,7 +238,7 @@
         (
             lax.all_to_all(forcing_vector_other, "col", split_axis=0, concat_axis=1, tiled=True),
             lax.all_to_all(mass_ratio_after, "col", split_axis=0, concat_axis=1, tiled=True),
-            lax.all_to_all(diffuse_thermal_energy, "col", split_axis=0, concat_axis=1, tiled=True),
+            swapped_with_each(diffuse_thermal_energy, "col", 0, 1),
         )
     )
     kelvin_after = lax.all_to_all(solved_state, "col", split_axis=1, concat_axis=0, tiled=True)

time: 667 us -> 664 us (level)
  waiting for transfers between devices: 310 us -> 279 us
  starting transfers between devices: 57.4 us -> 85.3 us
    ppermute x0 -> x7, starting transfers between devices: none -> 40.8 us  [swapped_with_each(): part = lax.ppermute(part, axis, [(d, d ^ mask) for d in range(ways)])]
    all_to_all x1 -> x0, starting transfers between devices: 19.4 us -> none  [per_device(): lax.all_to_all(diffuse_thermal_energy, 'col', split_axis=0, concat_axis=1...]
    all_to_all x1, waiting for transfers between devices: 18.6 us -> 0.01 us  [per_device(): lax.all_to_all(solved_x, 'row', split_axis=0, concat_axis=1, tiled=True)]
    all_to_all x1, waiting for transfers between devices: 11.8 us -> 0.01 us  [per_device(): lax.all_to_all(flat_parts[0], 'row', split_axis=1, concat_axis=0, tiled=T...]
    all_to_all x1, starting transfers between devices: 6.35 us -> 14.8 us  [per_device(): lax.all_to_all(solved_x, 'row', split_axis=0, concat_axis=1, tiled=True)]
  transfers between devices with their start and end apart: 8 -> 14, of which waited for: 8 -> 6; matrix products, arithmetic and copies ran while one was open for 5% -> 4% of each run, Pallas kernels for 0% -> 0%
where the time goes in v1:
time: 664 us; the launch traced here: 654 us
  waiting for transfers between devices  279 us (42%)
  other arithmetic  142 us (21%)
  local copies, waits for them, and re-layouts  121 us (18%)
  starting transfers between devices  85.3 us (13%)
  between operations  16.8 us (3%)
  blocking collectives  9.95 us (1%)
    unnamed x2, waiting for transfers between devices  237 us
    slice x177, local copies, waits for them, and re-layouts, take_part(): return lax.slice_in_dim(values, first_index, end_index, stride, solve_dim)  101 us
    scatter-add x1, other arithmetic, per_device(): jax.ops.segment_sum(flux_arriving.reshape(-1), flat_ids, num_segments=sou...  57.7 us
    scatter-add x1, other arithmetic, per_device(): jax.ops.segment_sum(blending_shares.reshape(-1), flat_ids, num_segments=s...  57.6 us
    ppermute x7, starting transfers between devices, swapped_with_each(): part = lax.ppermute(part, axis, [(d, d ^ mask) for d in range(ways)])  40.8 us
    all_to_all x1, starting transfers between devices, per_device(): lax.all_to_all(solved_x, 'row', split_axis=0, concat_axis=1, tiled=True)  14.8 us
    all_to_all x1, waiting for transfers between devices, per_device(): lax.all_to_all(flat_parts[1], 'row', split_axis=1, concat_axis=0, tiled=T...  14.6 us
    all_to_all x1, waiting for transfers between devices, per_device(): lax.all_to_all(flat_parts[2], 'row', split_axis=1, concat_axis=0, tiled=T...  13.8 us
  transfers between devices with their start and end apart: 14, of which 6 were waited for; matrix products, arithmetic and copies ran while one was open for 4% of the time, Pallas kernels for 0%

profile of v1, /device:TPU:1, one launch (start us, length us, event | category | flops | bytes accessed | tf_op | source)
XLA Modules:
  0.0 654.2 jit_solution(5641120072855570488)
XLA Ops:
  8.8 57.7 %scatter_custom_fusion = f32[32768]{0:T(1024)} fusion(s32[8192]{0:T(1024)S(1)} %bitcast.251, f32[8192]{0:T(1024)S(1)} %get-tuple-element.52, f32[]{:T(128)} %constant.82.clone.1), kind=kCustom, calls=%fused_computation.156 | custom fusion | flops 8192 | bytes 131076 | tf_op jit(solution)/shard_map/scatter-add | solution.py:201
  66.5 57.6 %scatter_custom_fusion.1 = f32[32768]{0:T(1024)} fusion(s32[8192]{0:T(1024)S(1)} %bitcast.252, f32[8192]{0:T(1024)S(1)} %get-tuple-element.53, f32[]{:T(128)} %constant.82.clone.1), kind=kCustom, calls=%fused_computation.154 | custom fusion | flops 8192 | bytes 131076 | tf_op jit(solution)/shard_map/scatter-add | solution.py:198
  125.6 4.5 slice.1020
  130.1 4.5 slice.1022
  134.7 4.5 slice.1033
  139.2 4.5 slice.1025
  145.7 236.8 %all-reduce.121.cloned.1.call-done = (f32[32768]{0:T(1024)}, f32[32768]{0:T(1024)}) async-done(((f32[32768]{0:T(1024)}, f32[32768]{0:T(1024)}), (f32[32768]{0:T(1024)}, f32[32768]{0:T(1024)})) %all-reduce.121.cloned.1.call-update) | async-done | bytes 262160
  383.9 4.5 slice.1024
  388.4 4.5 slice.1032
  393.4 4.5 slice.1017
  397.9 4.5 slice.1021
  405.3 3.0 slice.1030
  410.6 3.0 slice.1031
  421.2 3.0 slice.1044
  497.6 8.0 %all-to-all-start.1 = ((f32[8,64,128]{2,0,1:T(8,128)}), f32[8,64,128]{2,0,1:T(8,128)S(1)}, u32[]{:S(2)}, u32[]{:S(2)}) async-start(f32[8,64,128]{2,0,1:T(8,128)} %copy.570), calls=%async_computation.1 | async-start | bytes 524288 | tf_op jit(solution)/shard_map/all_to_all | solution.py:232
  507.4 13.8 %all-to-all-done.1 = f32[8,64,128]{2,0,1:T(8,128)S(1)} async-done(((f32[8,64,128]{2,0,1:T(8,128)}), f32[8,64,128]{2,0,1:T(8,128)S(1)}, u32[]{:S(2)}, u32[]{:S(2)}) %all-to-all-start.1) | async-done | bytes 262176 | tf_op jit(solution)/shard_map/all_to_all | solution.py:232
  521.2 6.2 all-to-all-start.2
  528.3 14.6 %all-to-all-done.2 = f32[8,64,128]{2,0,1:T(8,128)S(1)} async-done(((f32[8,64,128]{2,0,1:T(8,128)}), f32[8,64,128]{2,0,1:T(8,128)S(1)}, u32[]{:S(2)}, u32[]{:S(2)}) %all-to-all-start.2) | async-done | bytes 262176 | tf_op jit(solution)/shard_map/all_to_all | solution.py:231
  542.9 6.4 all-to-all-start
  549.4 15.9 %collective-permute-start = (f32[1,64,128]{2,1,0:T(8,128)S(1)}, f32[1,64,128]{2,1,0:T(8,128)S(1)}, u32[]{:S(2)}, u32[]{:S(2)}) collective-permute-start(f32[1,64,128]{2,1,0:T(8,128)S(1)} %get-tuple-element.98), channel_id=1, source_target_pairs={{0,1},{1,0},{2,3},{3,2},{4,5},{5,4},{6,7},{7,6},{8,9},{9,8},{10,11... | collective-permute-start | bytes 98312 | tf_op jit(solution)/shard_map/ppermute | solution.py:24
  569.0 14.8 %all-to-all-start.3 = ((f32[512,1,128]{2,1,0:T(1,128)}), f32[512,1,128]{2,1,0:T(1,128)S(1)}, u32[]{:S(2)}, u32[]{:S(2)}) async-start(f32[512,1,128]{2,1,0:T(1,128)} %bitcast.85), calls=%async_computation.3 | async-start | bytes 524288 | tf_op jit(solution)/shard_map/all_to_all | solution.py:235
  583.9 3.1 collective-permute-start.1
  587.1 8.0 %collective-permute-start.2 = (f32[1,64,128]{2,1,0:T(8,128)S(1)}, f32[1,64,128]{2,1,0:T(8,128)S(1)}, u32[]{:S(2)}, u32[]{:S(2)}) collective-permute-start(f32[1,64,128]{2,1,0:T(8,128)S(1)} %get-tuple-element.96), channel_id=1, source_target_pairs={{0,3},{1,2},{2,1},{3,0},{4,7},{5,6},{6,5},{7,4},{8,11},{9,10},{10,... | collective-permute-start | bytes 98312 | tf_op jit(solution)/shard_map/ppermute | solution.py:24
  595.1 4.6 collective-permute-start.3
  601.9 3.7 collective-permute-start.5
  605.6 3.3 collective-permute-start.6
  609.1 3.0 collective-permute-done.6
  612.1 4.6 all-to-all-start.5
  618.5 4.8 all-to-all-done.5
  623.3 4.4 all-to-all-start.4
  628.3 5.9 all-to-all-done.4
  636.5 9.9 %all_to_all.108 = f32[1,512,128]{2,0,1:T(1,128)S(1)} all-to-all(f32[1,512,128]{2,0,1:T(1,128)S(1)} %bitcast.220), channel_id=1, replica_groups=mesh['row'=64,'col'=8] {'col'}, dimensions={1} | all-to-all | bytes 524288 | tf_op jit(solution)/shard_map/all_to_all | solution.py:244
  (376 shorter events, 105.2 us)
Async XLA Ops:
  7.2 0.8 copy-start.16
  7.2 375.3 %all-reduce.121.cloned.1.call-start = ((), (), s32[]{:S(2)}) async-start(), calls=%async_computation.7 | async-start | bytes 524288
  7.9 0.8 copy-start.18
  8.8 116.2 %copy-start.11 = (f32[8,64,128]{2,1,0:T(8,128)S(1)}, f32[8,64,128]{2,1,0:T(8,128)}, u32[]{:S(2)}) copy-start(f32[8,64,128]{2,1,0:T(8,128)} %param.17) | copy-start | bytes 786436
  8.8 116.2 %copy-start.15 = (f32[8,64,128]{2,1,0:T(8,128)S(1)}, f32[8,64,128]{2,1,0:T(8,128)}, u32[]{:S(2)}) copy-start(f32[8,64,128]{2,1,0:T(8,128)} %param.16) | copy-start | bytes 786436
  473.1 1.1 copy-start.9
  476.9 1.0 copy-start.10
  479.7 2.0 copy-start.7
  479.7 2.0 copy-start.8
  481.7 4.1 copy-start.5
  481.7 4.1 copy-start.6
  483.8 2.0 copy-start.3
  483.8 2.0 copy-start.4
  487.7 0.9 copy-start.13
  488.7 1.0 copy-start.1
  488.7 1.0 copy-start.2
  488.9 1.0 copy-start
  490.8 0.9 copy-start.14
  493.5 1.0 copy-start.12
  497.6 23.6 %all-to-all-start.1 = ((f32[8,64,128]{2,0,1:T(8,128)}), f32[8,64,128]{2,0,1:T(8,128)S(1)}, u32[]{:S(2)}, u32[]{:S(2)}) async-start(f32[8,64,128]{2,0,1:T(8,128)} %copy.570), calls=%async_computation.1 | async-start | bytes 524288 | tf_op jit(solution)/shard_map/all_to_all | solution.py:232
  521.2 21.7 %all-to-all-start.2 = ((f32[8,64,128]{2,0,1:T(8,128)}), f32[8,64,128]{2,0,1:T(8,128)S(1)}, u32[]{:S(2)}, u32[]{:S(2)}) async-start(f32[8,64,128]{2,0,1:T(8,128)} %copy.571), calls=%async_computation.2 | async-start | bytes 524288 | tf_op jit(solution)/shard_map/all_to_all | solution.py:231
  542.9 23.1 %all-to-all-start = ((f32[8,64,128]{2,0,1:T(8,128)}), f32[8,64,128]{2,0,1:T(8,128)S(1)}, u32[]{:S(2)}, u32[]{:S(2)}) async-start(f32[8,64,128]{2,0,1:T(8,128)} %copy.569), calls=%async_computation | async-start | bytes 524288 | tf_op jit(solution)/shard_map/all_to_all | solution.py:230
  549.4 52.6 %collective-permute-start = (f32[1,64,128]{2,1,0:T(8,128)S(1)}, f32[1,64,128]{2,1,0:T(8,128)S(1)}, u32[]{:S(2)}, u32[]{:S(2)}) collective-permute-start(f32[1,64,128]{2,1,0:T(8,128)S(1)} %get-tuple-element.98), channel_id=1, source_target_pairs={{0,1},{1,0},{2,3},{3,2},{4,5},{5,4},{6,7},{7,6},{8,9},{9,8},{10,11... | collective-permute-start | bytes 98312 | tf_op jit(solution)/shard_map/ppermute | solution.py:24
  569.0 43.1 %all-to-all-start.3 = ((f32[512,1,128]{2,1,0:T(1,128)}), f32[512,1,128]{2,1,0:T(1,128)S(1)}, u32[]{:S(2)}, u32[]{:S(2)}) async-start(f32[512,1,128]{2,1,0:T(1,128)} %bitcast.85), calls=%async_computation.3 | async-start | bytes 524288 | tf_op jit(solution)/shard_map/all_to_all | solution.py:235
  583.9 21.7 %collective-permute-start.1 = (f32[1,64,128]{2,1,0:T(8,128)S(1)}, f32[1,64,128]{2,1,0:T(8,128)S(1)}, u32[]{:S(2)}, u32[]{:S(2)}) collective-permute-start(f32[1,64,128]{2,1,0:T(8,128)S(1)} %get-tuple-element.97), channel_id=1, source_target_pairs={{0,2},{1,3},{2,0},{3,1},{4,6},{5,7},{6,4},{7,5},{8,10},{9,11},{10,... | collective-permute-start | bytes 98312 | tf_op jit(solution)/shard_map/ppermute | solution.py:24
  587.1 21.9 %collective-permute-start.2 = (f32[1,64,128]{2,1,0:T(8,128)S(1)}, f32[1,64,128]{2,1,0:T(8,128)S(1)}, u32[]{:S(2)}, u32[]{:S(2)}) collective-permute-start(f32[1,64,128]{2,1,0:T(8,128)S(1)} %get-tuple-element.96), channel_id=1, source_target_pairs={{0,3},{1,2},{2,1},{3,0},{4,7},{5,6},{6,5},{7,4},{8,11},{9,10},{10,... | collective-permute-start | bytes 98312 | tf_op jit(solution)/shard_map/ppermute | solution.py:24
  595.1 14.0 %collective-permute-start.3 = (f32[1,64,128]{2,1,0:T(8,128)S(1)}, f32[1,64,128]{2,1,0:T(8,128)S(1)}, u32[]{:S(2)}, u32[]{:S(2)}) collective-permute-start(f32[1,64,128]{2,1,0:T(8,128)S(1)} %get-tuple-element.95), channel_id=1, source_target_pairs={{0,4},{1,5},{2,6},{3,7},{4,0},{5,1},{6,2},{7,3},{8,12},{9,13},{10,... | collective-permute-start | bytes 98312 | tf_op jit(solution)/shard_map/ppermute | solution.py:24
  599.7 9.3 %collective-permute-start.4 = (f32[1,64,128]{2,1,0:T(8,128)S(1)}, f32[1,64,128]{2,1,0:T(8,128)S(1)}, u32[]{:S(2)}, u32[]{:S(2)}) collective-permute-start(f32[1,64,128]{2,1,0:T(8,128)S(1)} %get-tuple-element.94), channel_id=1, source_target_pairs={{0,5},{1,4},{2,7},{3,6},{4,1},{5,0},{6,3},{7,2},{8,13},{9,12},{10,... | collective-permute-start | bytes 98312 | tf_op jit(solution)/shard_map/ppermute | solution.py:24
  601.9 7.2 %collective-permute-start.5 = (f32[1,64,128]{2,1,0:T(8,128)S(1)}, f32[1,64,128]{2,1,0:T(8,128)S(1)}, u32[]{:S(2)}, u32[]{:S(2)}) collective-permute-start(f32[1,64,128]{2,1,0:T(8,128)S(1)} %get-tuple-element.93), channel_id=1, source_target_pairs={{0,6},{1,7},{2,4},{3,5},{4,2},{5,3},{6,0},{7,1},{8,14},{9,15},{10,... | collective-permute-start | bytes 98312 | tf_op jit(solution)/shard_map/ppermute | solution.py:24
  605.6 6.4 collective-permute-start.6
  612.1 11.1 %all-to-all-start.5 = ((f32[8,64,128]{2,1,0:T(8,128)}), f32[8,64,128]{2,1,0:T(8,128)S(1)}, u32[]{:S(2)}, u32[]{:S(2)}) async-start(f32[8,64,128]{2,1,0:T(8,128)} %get-tuple-element.171), calls=%async_computation.5 | async-start | bytes 524288 | tf_op jit(solution)/shard_map/all_to_all | solution.py:240
  623.3 10.9 %all-to-all-start.4 = ((f32[8,64,128]{2,1,0:T(8,128)}), f32[8,64,128]{2,1,0:T(8,128)S(1)}, u32[]{:S(2)}, u32[]{:S(2)}) async-start(f32[8,64,128]{2,1,0:T(8,128)} %bitcast_multiply_fusion), calls=%async_computation.4 | async-start | bytes 524288 | tf_op jit(solution)/shard_map/all_to_all | solution.py:239
  (8 other events, 5.7 us)
Sparse Core Ops, SparseCore 0:
  124.3 258.1 all-reduce.120
